TPU v7x, 32 devices: a whole 2x2x4 slice. The times are simulated.
32 devices in a mesh: groups: 2 (over y), train: 4 (over z), layer: 4 (over x, core).
Axes of the slice: x: 2, y: 2, z: 4, core: 2. Of those that a mesh axis runs over, the one named last changes fastest.
Arguments:
- query_grads: bfloat16 [1024, 4, 4096], P('train', 'layer'), may hold values from -6 to 6
- train_grads: bfloat16 [8192, 4, 4096], P(('groups', 'train'), 'layer'), parts along dimension 0, may hold values from -0.046875 to 0.046875
- left_inverse: float32 [4, 64, 64], P('layer')
- right_inverse: float32 [4, 64, 64], P('layer')
- valid_rows: int32 [8], P(('groups', 'train')), parts along dimension 0, may hold values from 256 to 1024, as said below
- query_order: int32 [1024], replicated, may hold values from 0 to 1023, each once
Outputs:
- scores: float32 [1024, 8192], P('layer', ('groups', 'train')), parts along dimension 1
There are 2 independent parts, one for each index of `groups`. A program takes and returns all parts, laid end to end along the dimension named above; an argument that names none is the same for every part. Nothing has to cross between parts.
Inputs may be any that keep to these rules, and one draw needn't show every extreme that they name: `query_order`: a permutation: every query appears once. `valid_rows`: in every draw one shard has all 1024 slots live and another has 256.
All inputs are finite; a program needn't handle non-finite values.
Results may differ from a plain program's by a relative error of at most 0.0029.
Values may be sent and summed in bfloat16 or wider, within the bound.
A program may use at most 64 MiB of HBM per device.

v0:
```python
import jax
import jax.numpy as jnp
from jax import lax
from jax.sharding import PartitionSpec as P


def passed_along(block, axis, distance):
    devices = range(lax.axis_size(axis))
    route = [((i - distance) % len(devices), i) for i in devices]
    return lax.ppermute(block, axis, route)


def precondition(gradients, left_factor, right_factor):
    row_count = gradients.shape[0]
    layer_count = left_factor.shape[0]
    order_in = left_factor.shape[-1]
    order_out = right_factor.shape[-1]
    matrix = gradients.astype(jnp.float32).reshape(row_count, layer_count, order_in, order_out)
    matrix = jnp.einsum("lab,rlbc->rlac", left_factor, matrix, precision=lax.Precision.HIGHEST)
    matrix = jnp.einsum("rlac,lcd->rlad", matrix, right_factor, precision=lax.Precision.HIGHEST)
    return matrix.reshape(row_count, layer_count, order_in * order_out).astype(jnp.bfloat16)


def masked_scores(conditioned, train_flat, live_rows):
    slot_count = train_flat.shape[0]
    block_width = min(512, slot_count)
    query_count = conditioned.shape[0]
    pieces = []
    for first_row in range(0, slot_count, block_width):
        row_block = train_flat[first_row : first_row + block_width]

        def compute(row_block=row_block, first_row=first_row):
            product = lax.dot_general(
                conditioned, row_block, (((1,), (1,)), ((), ())), preferred_element_type=jnp.float32
            )
            live_mask = first_row + jnp.arange(block_width, dtype=jnp.int32) < live_rows
            return jnp.where(live_mask[None, :], product, jnp.zeros_like(product))

        def skipped():
            return jnp.zeros((query_count, block_width), jnp.float32)

        pieces.append(lax.cond(live_rows > first_row, compute, skipped))
    return jnp.concatenate(pieces, axis=1)


def body(query_grads, train_grads, left_inverse, right_inverse, valid_rows, query_order):
    cycle_size = lax.axis_size("train")
    position = lax.axis_index("train")
    block_rows = query_grads.shape[0]
    train_flat = train_grads.reshape(train_grads.shape[0], -1)
    live_rows = valid_rows[0]

    def score_block(moving):
        conditioned = precondition(moving, left_inverse, right_inverse)
        return masked_scores(conditioned.reshape(moving.shape[0], -1), train_flat, live_rows)

    def place(totals, moving, anchor):
        return lax.dynamic_update_slice_in_dim(totals, score_block(moving), anchor * block_rows, 0)

    empty_totals = jnp.zeros((block_rows * cycle_size, train_flat.shape[0]), jnp.float32)
    totals = place(empty_totals, query_grads, position)

    def turn(offset, state):
        moving, totals = state
        moving = passed_along(moving, "train", 1)
        return (moving, place(totals, moving, (position - offset) % cycle_size))

    moving, totals = lax.fori_loop(1, cycle_size, turn, (query_grads, totals))
    ordered = jnp.take(totals, query_order, axis=0)
    return lax.psum_scatter(ordered, "layer", scatter_dimension=0, tiled=True)


def solution(mesh):
    return jax.shard_map(
        body,
        mesh=mesh,
        in_specs=(
            P("train", "layer", None),
            P(("groups", "train"), "layer", None),
            P("layer", None, None),
            P("layer", None, None),
            P(("groups", "train")),
            P(),
        ),
        out_specs=P("layer", ("groups", "train")),
        check_vma=False,
    )
```

profile of v0, /device:TPU:0, one launch (start us, length us, event | category | flops | bytes accessed | tf_op | source)
XLA Modules:
  0.0 308.4 jit_solution(9622476820315844575)
XLA Ops:
  6.5 0.7 fusion.38
  7.2 0.7 compare_and_fusion
  7.9 4.1 %copy.28 = bf16[256,1,4096]{0,2,1:T(8,128)(2,1)} copy(bf16[256,1,4096]{2,0,1:T(8,128)(2,1)} %param.16) | data formatting | bytes 4194304 | tf_op jit(solution)/shard_map/while | solution.py:68
  12.1 4.3 %convolution_bitcast_fusion.1 = f32[256,64,64]{0,1,2:T(8,128)S(1)} fusion(bf16[256,64,64]{0,2,1:T(8,128)(2,1)} %bitcast.18, f32[1,64,64]{2,1,0:T(8,128)S(1)} %copy-done.1), kind=kOutput, calls=%fused_computation.29 | convolution fusion | flops 805306368 | bytes 6307840 | tf_op jit(solution)/shard_map/lab,rlbc->rlac/dot_general | solution.py:19
  16.4 5.8 %fusion.33 = bf16[256,64,64]{0,2,1:T(8,128)(2,1)S(1)} fusion(f32[256,64,64]{0,1,2:T(8,128)S(1)} %convolution_bitcast_fusion.1, f32[1,64,64]{2,1,0:T(8,128)S(1)} %copy-done.2), kind=kOutput, calls=%fused_computation.32 | convolution fusion | flops 806354944 | bytes 6307840 | tf_op jit(solution)/shard_map/rlac,lcd->rlad/dot_general | solution.py:20
  22.8 4.2 %conditional.4 = (f32[256,512]{1,0:T(8,128)S(1)}) conditional(s32[]{:T(128)} %convert_element_type.73, () %tuple.51, (s32[]{:T(128)}, bf16[1024,1,4096]{2,0,1:T(8,128)(2,1)}, bf16[256,4096]{0,1:T(8,128)(2,1)S(1)}) %tuple.95), branch_computations={%region_0.0_spmd, %region_1.2_spmd} | conditional | flops 1073873408 | bytes 6816780 | solution.py:42
  22.8 0.7 iota_compare_fusion
  23.5 3.6 %fusion.3 = f32[256,512]{1,0:T(8,128)S(1)} fusion(bf16[256,4096]{0,1:T(8,128)(2,1)S(1)} %get-tuple-element.314, bf16[1024,1,4096]{2,0,1:T(8,128)(2,1)} %get-tuple-element.261, pred[512]{0:T(512)(128)(4,1)S(1)} %iota_compare_fusion), kind=kOutput, calls=%fused_computation.4 | convolution fusion | flops 1073872896 | bytes 6816256 | tf_op jit(solution)/shard_map/cond/branch_1_fun/dot_general | solution.py:33
  27.0 4.4 %conditional.5 = (f32[256,512]{1,0:T(8,128)S(1)}) conditional(s32[]{:T(128)} %convert_element_type.79, () %tuple.53, (s32[]{:T(128)}, bf16[1024,1,4096]{2,0,1:T(8,128)(2,1)}, bf16[256,4096]{0,1:T(8,128)(2,1)S(1)}) %tuple.96), branch_computations={%region_2.3_spmd, %region_3.4_spmd} | conditional | flops 1073873920 | bytes 6816780 | solution.py:42
  27.0 0.7 add_compare_fusion
  27.7 3.6 %fusion.9 = f32[256,512]{1,0:T(8,128)S(1)} fusion(bf16[256,4096]{0,1:T(8,128)(2,1)S(1)} %get-tuple-element.317, bf16[1024,1,4096]{2,0,1:T(8,128)(2,1)} %get-tuple-element.264, pred[512]{0:T(512)(128)(4,1)S(1)} %add_compare_fusion), kind=kOutput, calls=%fused_computation.9 | convolution fusion | flops 1073872896 | bytes 6816256 | tf_op jit(solution)/shard_map/cond/branch_1_fun/dot_general | solution.py:33
  32.1 1.9 copy-done
  34.0 212.0 %while.17 = (s32[]{:T(128)}, bf16[256,1,4096]{0,2,1:T(8,128)(2,1)}, f32[1024,1024]{1,0:T(8,128)}, pred[]{:T(512)}, f32[1,64,64]{2,1,0:T(8,128)S(1)}, /*index=5*/...) while((s32[]{:T(128)}, bf16[256,1,4096]{0,2,1:T(8,128)(2,1)}, ...), condition=%wide.region_9.10_spmd, body=%wide.region_4.9_spmd.sunk | while | flops 3759670784 | bytes 40929720 | solution.py:68
  34.0 50.9 %collective-permute-done = bf16[256,1,4096]{0,2,1:T(8,128)(2,1)S(1)} collective-permute-done((bf16[256,1,4096]{0,2,1:T(8,128)(2,1)}, bf16[256,1,4096]{0,2,1:T(8,128)(2,1)S(1)}, u32[]{:S(2)}, u32[]{:S(2)}) %collective-permute-start) | collective-permute-done | bytes 2097184 | tf_op jit(solution)/shard_map/while/body/eval_jaxpr/ppermute | solution.py:10
  84.9 2.7 convolution_bitcast_fusion.3
  87.6 6.8 %fusion.52 = bf16[256,64,64]{0,2,1:T(8,128)(2,1)} fusion(f32[256,64,64]{0,1,2:T(8,128)S(1)} %convolution_bitcast_fusion.3, f32[1,64,64]{1,2,0:T(8,128)S(1)} %get-tuple-element.446), kind=kOutput, calls=%fused_computation.23.clone.1 | convolution fusion | flops 806354944 | bytes 6307840 | tf_op jit(solution)/shard_map/while/body/eval_jaxpr/rlac,lcd->rlad/dot_general | solution.py:20
  94.4 4.8 %conditional.8 = (f32[256,512]{1,0:T(8,128)S(1)}) conditional(s32[]{:T(128)} %convert_element_type.86, () %tuple.76, (s32[]{:T(128)}, bf16[1024,4096]{1,0:T(8,128)(2,1)}, bf16[256,4096]{0,1:T(8,128)(2,1)}) %tuple.93), branch_computations={%region_7.7_spmd, %region_8.8_spmd} | conditional | flops 1073873920 | bytes 6816780 | solution.py:42
  94.4 0.7 add_compare_fusion.1
  95.0 4.1 %fusion.19 = f32[256,512]{1,0:T(8,128)S(1)} fusion(bf16[256,4096]{0,1:T(8,128)(2,1)} %get-tuple-element.311, bf16[1024,4096]{1,0:T(8,128)(2,1)} %get-tuple-element.270, pred[512]{0:T(512)(128)(4,1)S(1)} %add_compare_fusion.1), kind=kOutput, calls=%fused_computation.17 | convolution fusion | flops 1073872896 | bytes 6816256 | tf_op jit(solution)/shard_map/while/body/eval_jaxpr/cond/branch_1_fun/dot_general | solution.py:33
  99.2 4.8 %conditional.9 = (f32[256,512]{1,0:T(8,128)S(1)}) conditional(s32[]{:T(128)} %convert_element_type.87, () %tuple.78, (s32[]{:T(128)}, bf16[1024,4096]{1,0:T(8,128)(2,1)}, bf16[256,4096]{0,1:T(8,128)(2,1)}) %tuple.94), branch_computations={%region_5.5_spmd, %region_6.6_spmd} | conditional | flops 1073873408 | bytes 6816780 | solution.py:42
  99.2 0.7 iota_compare_fusion.1
  99.9 4.1 %fusion.14 = f32[256,512]{1,0:T(8,128)S(1)} fusion(bf16[256,4096]{0,1:T(8,128)(2,1)} %get-tuple-element.308, bf16[1024,4096]{1,0:T(8,128)(2,1)} %get-tuple-element.267, pred[512]{0:T(512)(128)(4,1)S(1)} %iota_compare_fusion.1), kind=kOutput, calls=%fused_computation.13 | convolution fusion | flops 1073872896 | bytes 6816256 | tf_op jit(solution)/shard_map/while/body/eval_jaxpr/cond/branch_1_fun/dot_general | solution.py:33
  104.0 1.1 maximum_dynamic-update-slice_fusion.3
  105.1 1.3 copy.69
  106.4 48.8 %collective-permute-done = bf16[256,1,4096]{0,2,1:T(8,128)(2,1)S(1)} collective-permute-done((bf16[256,1,4096]{0,2,1:T(8,128)(2,1)}, bf16[256,1,4096]{0,2,1:T(8,128)(2,1)S(1)}, u32[]{:S(2)}, u32[]{:S(2)}) %collective-permute-start) | collective-permute-done | bytes 2097184 | tf_op jit(solution)/shard_map/while/body/eval_jaxpr/ppermute | solution.py:10
  155.2 2.7 convolution_bitcast_fusion.3
  157.9 6.8 %fusion.52 = bf16[256,64,64]{0,2,1:T(8,128)(2,1)} fusion(f32[256,64,64]{0,1,2:T(8,128)S(1)} %convolution_bitcast_fusion.3, f32[1,64,64]{1,2,0:T(8,128)S(1)} %get-tuple-element.446), kind=kOutput, calls=%fused_computation.23.clone.1 | convolution fusion | flops 806354944 | bytes 6307840 | tf_op jit(solution)/shard_map/while/body/eval_jaxpr/rlac,lcd->rlad/dot_general | solution.py:20
  164.7 4.8 %conditional.8 = (f32[256,512]{1,0:T(8,128)S(1)}) conditional(s32[]{:T(128)} %convert_element_type.86, () %tuple.76, (s32[]{:T(128)}, bf16[1024,4096]{1,0:T(8,128)(2,1)}, bf16[256,4096]{0,1:T(8,128)(2,1)}) %tuple.93), branch_computations={%region_7.7_spmd, %region_8.8_spmd} | conditional | flops 1073873920 | bytes 6816780 | solution.py:42
  164.7 0.7 add_compare_fusion.1
  165.3 4.1 %fusion.19 = f32[256,512]{1,0:T(8,128)S(1)} fusion(bf16[256,4096]{0,1:T(8,128)(2,1)} %get-tuple-element.311, bf16[1024,4096]{1,0:T(8,128)(2,1)} %get-tuple-element.270, pred[512]{0:T(512)(128)(4,1)S(1)} %add_compare_fusion.1), kind=kOutput, calls=%fused_computation.17 | convolution fusion | flops 1073872896 | bytes 6816256 | tf_op jit(solution)/shard_map/while/body/eval_jaxpr/cond/branch_1_fun/dot_general | solution.py:33
  169.5 4.8 %conditional.9 = (f32[256,512]{1,0:T(8,128)S(1)}) conditional(s32[]{:T(128)} %convert_element_type.87, () %tuple.78, (s32[]{:T(128)}, bf16[1024,4096]{1,0:T(8,128)(2,1)}, bf16[256,4096]{0,1:T(8,128)(2,1)}) %tuple.94), branch_computations={%region_5.5_spmd, %region_6.6_spmd} | conditional | flops 1073873408 | bytes 6816780 | solution.py:42
  169.5 0.7 iota_compare_fusion.1
  170.1 4.1 %fusion.14 = f32[256,512]{1,0:T(8,128)S(1)} fusion(bf16[256,4096]{0,1:T(8,128)(2,1)} %get-tuple-element.308, bf16[1024,4096]{1,0:T(8,128)(2,1)} %get-tuple-element.267, pred[512]{0:T(512)(128)(4,1)S(1)} %iota_compare_fusion.1), kind=kOutput, calls=%fused_computation.13 | convolution fusion | flops 1073872896 | bytes 6816256 | tf_op jit(solution)/shard_map/while/body/eval_jaxpr/cond/branch_1_fun/dot_general | solution.py:33
  174.3 1.0 maximum_dynamic-update-slice_fusion.3
  175.3 1.3 copy.69
  176.6 47.9 %collective-permute-done = bf16[256,1,4096]{0,2,1:T(8,128)(2,1)S(1)} collective-permute-done((bf16[256,1,4096]{0,2,1:T(8,128)(2,1)}, bf16[256,1,4096]{0,2,1:T(8,128)(2,1)S(1)}, u32[]{:S(2)}, u32[]{:S(2)}) %collective-permute-start) | collective-permute-done | bytes 2097184 | tf_op jit(solution)/shard_map/while/body/eval_jaxpr/ppermute | solution.py:10
  224.5 2.7 convolution_bitcast_fusion.3
  227.2 6.8 %fusion.52 = bf16[256,64,64]{0,2,1:T(8,128)(2,1)} fusion(f32[256,64,64]{0,1,2:T(8,128)S(1)} %convolution_bitcast_fusion.3, f32[1,64,64]{1,2,0:T(8,128)S(1)} %get-tuple-element.446), kind=kOutput, calls=%fused_computation.23.clone.1 | convolution fusion | flops 806354944 | bytes 6307840 | tf_op jit(solution)/shard_map/while/body/eval_jaxpr/rlac,lcd->rlad/dot_general | solution.py:20
  234.0 4.8 %conditional.8 = (f32[256,512]{1,0:T(8,128)S(1)}) conditional(s32[]{:T(128)} %convert_element_type.86, () %tuple.76, (s32[]{:T(128)}, bf16[1024,4096]{1,0:T(8,128)(2,1)}, bf16[256,4096]{0,1:T(8,128)(2,1)}) %tuple.93), branch_computations={%region_7.7_spmd, %region_8.8_spmd} | conditional | flops 1073873920 | bytes 6816780 | solution.py:42
  234.7 4.1 %fusion.19 = f32[256,512]{1,0:T(8,128)S(1)} fusion(bf16[256,4096]{0,1:T(8,128)(2,1)} %get-tuple-element.311, bf16[1024,4096]{1,0:T(8,128)(2,1)} %get-tuple-element.270, pred[512]{0:T(512)(128)(4,1)S(1)} %add_compare_fusion.1), kind=kOutput, calls=%fused_computation.17 | convolution fusion | flops 1073872896 | bytes 6816256 | tf_op jit(solution)/shard_map/while/body/eval_jaxpr/cond/branch_1_fun/dot_general | solution.py:33
  238.8 4.8 %conditional.9 = (f32[256,512]{1,0:T(8,128)S(1)}) conditional(s32[]{:T(128)} %convert_element_type.87, () %tuple.78, (s32[]{:T(128)}, bf16[1024,4096]{1,0:T(8,128)(2,1)}, bf16[256,4096]{0,1:T(8,128)(2,1)}) %tuple.94), branch_computations={%region_5.5_spmd, %region_6.6_spmd} | conditional | flops 1073873408 | bytes 6816780 | solution.py:42
  238.8 0.7 iota_compare_fusion.1
  239.5 4.1 %fusion.14 = f32[256,512]{1,0:T(8,128)S(1)} fusion(bf16[256,4096]{0,1:T(8,128)(2,1)} %get-tuple-element.308, bf16[1024,4096]{1,0:T(8,128)(2,1)} %get-tuple-element.267, pred[512]{0:T(512)(128)(4,1)S(1)} %iota_compare_fusion.1), kind=kOutput, calls=%fused_computation.13 | convolution fusion | flops 1073872896 | bytes 6816256 | tf_op jit(solution)/shard_map/while/body/eval_jaxpr/cond/branch_1_fun/dot_general | solution.py:33
  243.6 1.1 maximum_dynamic-update-slice_fusion.3
  244.7 1.3 copy.69
  246.0 8.6 %gather_fusion = f32[1024,1024]{1,0:T(8,128)} fusion(f32[1024,1024]{1,0:T(8,128)} %get-tuple-element.283, s32[1024]{0:T(1024)S(1)} %fusion.38), kind=kCustom, calls=%fused_computation | custom fusion | bytes 8392704 | tf_op jit(solution)/shard_map/jit(_take)/gather | solution.py:69
  254.6 4.5 %broadcast_select_fusion = f32[1024,1024]{1,0:T(8,128)} fusion(f32[1024,1024]{1,0:T(8,128)} %gather_fusion, pred[1024]{0:T(1024)(128)(4,1)S(1)} %compare_and_fusion), kind=kLoop, calls=%fused_computation.31 | loop fusion | flops 1048576 | bytes 8389632 | tf_op jit(solution)/shard_map/jit(_take)/select_n | solution.py:69
  259.2 42.4 %reduce-scatter.2.cloned.1.call-done = f32[256,1024]{1,0:T(8,128)} async-done(((f32[1024,1024]{1,0:T(8,128)}), f32[256,1024]{1,0:T(8,128)}) %reduce-scatter.2.cloned.1.call-update) | async-done | bytes 1048592 | tf_op jit(solution)/shard_map/reduce_scatter | solution.py:70
  (14 shorter events, 1.4 us)
Async XLA Ops:
  6.5 5.5 %copy-start.2 = (f32[1,64,64]{2,1,0:T(8,128)S(1)}, f32[1,64,64]{2,1,0:T(8,128)}, u32[]{:S(2)}) copy-start(f32[1,64,64]{2,1,0:T(8,128)} %param.19) | copy-start | bytes 49156
  6.5 5.5 %copy-start.1 = (f32[1,64,64]{2,1,0:T(8,128)S(1)}, f32[1,64,64]{2,1,0:T(8,128)}, u32[]{:S(2)}) copy-start(f32[1,64,64]{2,1,0:T(8,128)} %param.18) | copy-start | bytes 49156
  6.5 295.0 %reduce-scatter.2.cloned.1.call-start = ((), (), s32[]{:S(2)}) async-start(), calls=%async_computation.1 | async-start | bytes 5242880 | tf_op jit(solution)/shard_map/reduce_scatter | solution.py:70
  32.1 1.9 copy-start
  34.0 50.9 %collective-permute-start = (bf16[256,1,4096]{0,2,1:T(8,128)(2,1)}, bf16[256,1,4096]{0,2,1:T(8,128)(2,1)S(1)}, u32[]{:S(2)}, u32[]{:S(2)}) collective-permute-start(bf16[256,1,4096]{0,2,1:T(8,128)(2,1)} %get-tuple-element.426), channel_id=1, source_target_pairs={{12,0},{0,4},{4,8},{8,12},{13,1},{1,5},{5,9},{9,13},{14,2},{2,6},{... | collective-permute-start | bytes 6291464 | tf_op jit(solution)/shard_map/while/body/eval_jaxpr/ppermute | solution.py:10
  106.4 48.8 %collective-permute-start = (bf16[256,1,4096]{0,2,1:T(8,128)(2,1)}, bf16[256,1,4096]{0,2,1:T(8,128)(2,1)S(1)}, u32[]{:S(2)}, u32[]{:S(2)}) collective-permute-start(bf16[256,1,4096]{0,2,1:T(8,128)(2,1)} %get-tuple-element.426), channel_id=1, source_target_pairs={{12,0},{0,4},{4,8},{8,12},{13,1},{1,5},{5,9},{9,13},{14,2},{2,6},{... | collective-permute-start | bytes 6291464 | tf_op jit(solution)/shard_map/while/body/eval_jaxpr/ppermute | solution.py:10
  176.6 47.9 %collective-permute-start = (bf16[256,1,4096]{0,2,1:T(8,128)(2,1)}, bf16[256,1,4096]{0,2,1:T(8,128)(2,1)S(1)}, u32[]{:S(2)}, u32[]{:S(2)}) collective-permute-start(bf16[256,1,4096]{0,2,1:T(8,128)(2,1)} %get-tuple-element.426), channel_id=1, source_target_pairs={{12,0},{0,4},{4,8},{8,12},{13,1},{1,5},{5,9},{9,13},{14,2},{2,6},{... | collective-permute-start | bytes 6291464 | tf_op jit(solution)/shard_map/while/body/eval_jaxpr/ppermute | solution.py:10
Sparse Core Ops, SparseCore 0:
  259.3 42.1 reduce-scatter.1
where the time goes:
time: 309 us; the launch traced here: 308 us
  waiting for transfers between devices  190 us (61%)
  matrix products  70.2 us (23%)
  local copies, waits for them, and re-layouts  19.2 us (6%)
  other arithmetic  14.4 us (5%)
  between operations  14.1 us (5%)
    ppermute x3, waiting for transfers between devices, passed_along(): return lax.ppermute(block, axis, route)  148 us
    reduce_scatter x1, waiting for transfers between devices, body(): return lax.psum_scatter(ordered, 'layer', scatter_dimension=0, tiled=True)  42.4 us
    dot_general x8, matrix products, compute(): lax.dot_general(conditioned, row_block, (((1,), (1,)), ((), ())), preferr...  31.8 us
    dot_general x4, matrix products, precondition(): jnp.einsum('rlac,lcd->rlad', matrix, right_factor, precision=lax.Precisio...  26 us
    dot_general x4, matrix products, precondition(): jnp.einsum('lab,rlbc->rlac', left_factor, matrix, precision=lax.Precision...  12.3 us
    gather x1, local copies, waits for them, and re-layouts, body(): ordered = jnp.take(totals, query_order, axis=0)  8.61 us
  transfers between devices with their start and end apart: 4, of which 4 were waited for; matrix products, arithmetic and copies ran while one was open for 0% of the time, Pallas kernels for 0%

commit v1 on v0

v1 whole, which is shorter than its diff:
```python
import jax
import jax.numpy as jnp
from jax import lax
from jax.sharding import PartitionSpec as P


def precondition(gradients, left_factor, right_factor):
    row_count = gradients.shape[0]
    layer_count = left_factor.shape[0]
    order_in = left_factor.shape[-1]
    order_out = right_factor.shape[-1]
    matrix = gradients.astype(jnp.float32).reshape(row_count, layer_count, order_in, order_out)
    matrix = jnp.einsum("lab,rlbc->rlac", left_factor, matrix, precision=lax.Precision.HIGHEST)
    matrix = jnp.einsum("rlac,lcd->rlad", matrix, right_factor, precision=lax.Precision.HIGHEST)
    return matrix.reshape(row_count, layer_count, order_in * order_out).astype(jnp.bfloat16)


def summed_over_layers(partial):
    size = lax.axis_size("layer")
    me = lax.axis_index("layer")
    columns = partial.shape[-1]
    blocks = partial.reshape(size, -1, columns)
    step = 1
    while step < size:
        count = size // step
        halves = blocks.reshape(count // 2, 2, -1, columns)
        bit = (me // step) % 2
        kept = lax.dynamic_index_in_dim(halves, bit, 1, keepdims=False)
        given = lax.dynamic_index_in_dim(halves, 1 - bit, 1, keepdims=False)
        if step > 1:
            given = given.astype(jnp.bfloat16)
        route = [(i, i ^ step) for i in range(size)]
        taken = lax.ppermute(given, "layer", route)
        blocks = kept + taken.astype(jnp.float32)
        step *= 2
    return blocks.reshape(-1, columns)


def body(query_grads, train_grads, left_inverse, right_inverse, valid_rows, query_order):
    groups = lax.axis_size("groups")
    share = query_grads.shape[0] // groups
    own = lax.dynamic_slice_in_dim(query_grads, lax.axis_index("groups") * share, share, 0)
    conditioned = precondition(own, left_inverse, right_inverse).reshape(share, -1)
    conditioned = lax.all_gather(conditioned, ("train", "groups"), axis=0, tiled=True)
    train_flat = train_grads.reshape(train_grads.shape[0], -1)
    product = lax.dot_general(
        conditioned, train_flat, (((1,), (1,)), ((), ())), preferred_element_type=jnp.float32
    )
    live = jnp.arange(train_flat.shape[0], dtype=jnp.int32) < valid_rows[0]
    product = jnp.where(live[None, :], product, 0.0)
    ordered = jnp.take(product, query_order, axis=0)
    return summed_over_layers(ordered)


def solution(mesh):
    return jax.shard_map(
        body,
        mesh=mesh,
        in_specs=(
            P("train", "layer", None),
            P(("groups", "train"), "layer", None),
            P("layer", None, None),
            P("layer", None, None),
            P(("groups", "train")),
            P(),
        ),
        out_specs=P("layer", ("groups", "train")),
        check_vma=False,
    )
```

time: 309 us -> 207 us (0.67)
  matrix products: 70.2 us -> 20.8 us
  waiting for transfers between devices: 190 us -> 145 us
  other arithmetic: 14.4 us -> 7.55 us
    ppermute x3 -> x2, waiting for transfers between devices: 148 us -> 17 us  [summed_over_layers(): taken = lax.ppermute(given, 'layer', route)]
    all_gather x0 -> x1, waiting for transfers between devices: none -> 128 us  [body(): lax.all_gather(conditioned, ('train', 'groups'), axis=0, tiled=True)]
    reduce_scatter x1 -> x0, waiting for transfers between devices: 42.4 us -> none  [body(): return lax.psum_scatter(ordered, 'layer', scatter_dimension=0, tiled=True)]
    dot_general x4 -> x1, matrix products: 26 us -> 4.25 us  [precondition(): jnp.einsum('rlac,lcd->rlad', matrix, right_factor, precision=lax.Precisio...]
    dot_general x8 -> x1, matrix products: 31.8 us -> 15.2 us  [body(): lax.dot_general(conditioned, train_flat, (((1,), (1,)), ((), ())), prefer...]
    dot_general x4 -> x1, matrix products: 12.3 us -> 1.41 us  [precondition(): jnp.einsum('lab,rlbc->rlac', left_factor, matrix, precision=lax.Precision...]
    while x5 -> x0, local copies, waits for them, and re-layouts: 8.14 us -> none  [the longest x2 4.14 us: body(): moving, totals = lax.fori_loop(1, cycle_size, turn, (query_grads, totals))]
    lt x8 -> x1, other arithmetic: 5.21 us -> 0.01 us  [body(): live = jnp.arange(train_flat.shape[0], dtype=jnp.int32) < valid_rows[0]]
  transfers between devices with their start and end apart: 4 -> 3, of which waited for: 4 -> 3; matrix products, arithmetic and copies ran while one was open for 0% -> 0% of each run, Pallas kernels for 0% -> 0%
where the time goes in v1:
time: 207 us; the launch traced here: 206 us
  waiting for transfers between devices  145 us (70%)
  matrix products  20.8 us (10%)
  local copies, waits for them, and re-layouts  17.7 us (9%)
  between operations  14.2 us (7%)
  other arithmetic  7.55 us (4%)
    all_gather x1, waiting for transfers between devices, body(): lax.all_gather(conditioned, ('train', 'groups'), axis=0, tiled=True)  128 us
    ppermute x2, waiting for transfers between devices, summed_over_layers(): taken = lax.ppermute(given, 'layer', route)  17 us
    dot_general x1, matrix products, body(): lax.dot_general(conditioned, train_flat, (((1,), (1,)), ((), ())), prefer...  15.2 us
    gather x1, local copies, waits for them, and re-layouts, body(): ordered = jnp.take(product, query_order, axis=0)  8.57 us
    unnamed x13, local copies, waits for them, and re-layouts  6.47 us
    dot_general x1, matrix products, precondition(): jnp.einsum('rlac,lcd->rlad', matrix, right_factor, precision=lax.Precisio...  4.25 us
  transfers between devices with their start and end apart: 3, of which 3 were waited for; matrix products, arithmetic and copies ran while one was open for 0% of the time, Pallas kernels for 0%

profile of v1, /device:TPU:0, one launch (start us, length us, event | category | flops | bytes accessed | tf_op | source)
XLA Modules:
  0.0 206.3 jit_solution(7714881548243508894)
XLA Ops:
  6.5 0.0 copy-start
  6.5 0.0 copy-start.3
  6.5 0.0 copy-start.4
  6.5 0.0 all-gather.2.cloned.1.call-start
  6.6 1.6 copy-done
  8.1 1.1 constant_dynamic-slice_fusion
  9.2 1.6 copy.15
  10.8 0.0 copy-start.5
  10.8 0.0 copy-done.3
  10.8 1.4 convolution_bitcast_fusion
  12.3 0.0 copy-done.4
  12.3 4.2 %fusion.7 = bf16[128,64,64]{0,2,1:T(8,128)(2,1)} fusion(f32[128,64,64]{0,1,2:T(8,128)S(1)} %convolution_bitcast_fusion, f32[1,64,64]{2,1,0:T(8,128)S(1)} %copy-done.4), kind=kOutput, calls=%fused_computation.10 | convolution fusion | flops 403177472 | bytes 3162112 | tf_op jit(solution)/shard_map/rlac,lcd->rlad/dot_general | solution.py:14
  16.5 0.0 all-gather.2.cloned.1.call-update
  17.2 0.0 copy-done.5
  17.3 127.5 %all-gather.2.cloned.1.call-done = bf16[1024,4096]{0,1:T(8,128)(2,1)} async-done(((bf16[128,4096]{0,1:T(8,128)(2,1)}), bf16[1024,4096]{0,1:T(8,128)(2,1)}) %all-gather.2.cloned.1.call-update) | async-done | bytes 8388624 | tf_op jit(solution)/shard_map/all_gather | solution.py:44
  144.8 15.2 %fusion.2 = f32[1024,1024]{1,0:T(8,128)} fusion(bf16[1024,4096]{0,1:T(8,128)(2,1)} %all-gather.2.cloned.1.call-done, bf16[1024,1,4096]{2,0,1:T(8,128)(2,1)} %param.7, pred[1024]{0:T(1024)(128)(4,1)S(1)} %iota_compare_fusion), kind=kOutput, calls=%fused_computation.3 | convolution fusion | flops 8590983168 | bytes 20972544 | tf_op jit(solution)/shard_map/dot_general | solution.py:46
  159.9 8.6 %gather_fusion = f32[1024,1024]{1,0:T(8,128)} fusion(f32[1024,1024]{1,0:T(8,128)} %fusion.2, s32[1024]{0:T(1024)S(1)} %fusion.13), kind=kCustom, calls=%fused_computation | custom fusion | bytes 8392704 | tf_op jit(solution)/shard_map/jit(_take)/gather | solution.py:51
  168.5 2.5 %broadcast_select_fusion = f32[2,2,256,1024]{3,2,1,0:T(8,128)S(1)} fusion(f32[2,2,256,1024]{3,2,1,0:T(8,128)} %bitcast.38, pred[2,2,256]{2,1,0:T(4,128)(4,1)S(1)} %broadcast_in_dim.27), kind=kLoop, calls=%fused_computation.8 | loop fusion | flops 1048576 | bytes 8389632 | tf_op jit(solution)/shard_map/jit(_take)/select_n | solution.py:51
  171.1 0.0 copy-start.1
  171.1 1.9 copy-done.1
  173.0 1.5 dynamic-slice_bitcast_fusion
  174.5 0.0 collective-permute-start
  174.5 4.5 %collective-permute-done = f32[2,256,1024]{2,1,0:T(8,128)} collective-permute-done((f32[2,256,1024]{2,1,0:T(8,128)}, f32[2,256,1024]{2,1,0:T(8,128)}, u32[]{:S(2)}, u32[]{:S(2)}) %collective-permute-start) | collective-permute-done | bytes 2097184 | tf_op jit(solution)/shard_map/ppermute | solution.py:33
  179.0 2.6 %bitcast_add_fusion = f32[2,256,1024]{2,1,0:T(8,128)S(1)} fusion(f32[2,256,1024]{2,1,0:T(8,128)} %collective-permute-done, f32[2,2,256,1024]{3,2,1,0:T(8,128)} %copy-done.1, s32[]{:T(128)S(6)} %select_n.52), kind=kLoop, calls=%fused_computation.4 | loop fusion | flops 524288 | bytes 6291460 | tf_op jit(solution)/shard_map/add | solution.py:34
  181.6 0.0 copy-start.2
  181.6 1.3 copy-done.2
  182.9 0.1 dynamic-slice_convert_fusion
  183.0 1.5 collective-permute-start.1
  184.6 12.5 %collective-permute-done.1 = bf16[1,256,1024]{2,1,0:T(8,128)(2,1)S(1)} collective-permute-done((bf16[1,256,1024]{2,1,0:T(8,128)(2,1)S(1)}, bf16[1,256,1024]{2,1,0:T(8,128)(2,1)S(1)}, u32[]{:S(2)}, u32[]{:S(2)}) %collective-permute-start.1) | collective-permute-done | bytes 524320 | tf_op jit(solution)/shard_map/ppermute | solution.py:33
  197.1 2.4 %add_bitcast_fusion = f32[256,1024]{1,0:T(8,128)} fusion(bf16[1,256,1024]{2,1,0:T(8,128)(2,1)S(1)} %collective-permute-done.1, f32[2,256,1024]{2,1,0:T(8,128)} %copy-done.2, s32[]{:T(128)S(6)} %select_n.56), kind=kLoop, calls=%fused_computation.12 | loop fusion | flops 524288 | bytes 2621444 | tf_op jit(solution)/shard_map/reshape | solution.py:36
  (4 shorter events, 0.0 us)
Async XLA Ops:
  6.5 1.6 copy-start
  6.5 4.3 %copy-start.3 = (f32[1,64,64]{2,1,0:T(8,128)S(1)}, f32[1,64,64]{2,1,0:T(8,128)}, u32[]{:S(2)}) copy-start(f32[1,64,64]{2,1,0:T(8,128)} %param.8) | copy-start | bytes 49156
  6.5 5.7 %copy-start.4 = (f32[1,64,64]{2,1,0:T(8,128)S(1)}, f32[1,64,64]{2,1,0:T(8,128)}, u32[]{:S(2)}) copy-start(f32[1,64,64]{2,1,0:T(8,128)} %param.9) | copy-start | bytes 49156
  6.5 138.2 %all-gather.2.cloned.1.call-start = ((), (), s32[]{:S(2)}) async-start(), calls=%async_computation | async-start | bytes 9437184 | tf_op jit(solution)/shard_map/all_gather | solution.py:44
  10.8 6.4 %copy-start.5 = (s32[1024]{0:T(1024)S(1)}, s32[1024]{0:T(1024)}, u32[]{:S(2)}) copy-start(s32[1024]{0:T(1024)} %param.11) | copy-start | bytes 12292
  171.1 1.9 copy-start.1
  174.5 4.5 %collective-permute-start = (f32[2,256,1024]{2,1,0:T(8,128)}, f32[2,256,1024]{2,1,0:T(8,128)}, u32[]{:S(2)}, u32[]{:S(2)}) collective-permute-start(f32[2,256,1024]{2,1,0:T(8,128)} %dynamic-slice_bitcast_fusion), channel_id=1, source_target_pairs={{0,1},{1,0},{2,3},{3,2},{4,5},{5,4},{6,7},{7,6},{8,9},{9,8},{10,11... | collective-permute-start | bytes 6291464 | tf_op jit(solution)/shard_map/ppermute | solution.py:33
  181.6 1.3 copy-start.2
  183.0 14.0 %collective-permute-start.1 = (bf16[1,256,1024]{2,1,0:T(8,128)(2,1)S(1)}, bf16[1,256,1024]{2,1,0:T(8,128)(2,1)S(1)}, u32[]{:S(2)}, u32[]{:S(2)}) collective-permute-start(bf16[1,256,1024]{2,1,0:T(8,128)(2,1)S(1)} %dynamic-slice_convert_fusion), channel_id=1, source_target_pairs={{0,2},{1,3},{2,0},{3,1},{4,6},{5,7},{6,4},{7,5},{8,10},{9,11},{10,... | collective-permute-start | bytes 1572872 | tf_op jit(solution)/shard_map/ppermute | solution.py:33
Sparse Core Ops, SparseCore 0:
  16.7 128.0 all-gather.1

commit v2 on v1

--- a/solution.py
+++ b/solution.py
@@ -1,6 +1,10 @@
+import functools
+
 import jax
 import jax.numpy as jnp
 from jax import lax
+from jax.experimental import pallas as pl
+from jax.experimental.pallas import tpu as pltpu
 from jax.sharding import PartitionSpec as P
 
 
@@ -36,20 +40,172 @@
     return blocks.reshape(-1, columns)
 
 
+def gather_and_score(cycle, chunks, own_ref, train_ref, product_ref, gathered, train, z_send, z_recv, y_send, y_recv, train_sem):
+    position = lax.axis_index("train")
+    group = lax.axis_index("groups")
+    block = own_ref.shape[0]
+    share = block // 2
+    rows = share // chunks
+    width = train.shape[0] // chunks
+    load = pltpu.make_async_copy(train_ref, train, train_sem)
+    load.start()
+
+    has = (position > 0, position < cycle - 1)
+    neighbour = ((position + cycle - 1) % cycle, (position + 1) % cycle)
+    other = 1 - group
+    barrier = pltpu.get_barrier_semaphore()
+    for side in range(2):
+
+        @pl.when(has[side])
+        def _(side=side):
+            pl.semaphore_signal(barrier, inc=1, device_id={"train": neighbour[side]}, device_id_type=pl.DeviceIdType.MESH)
+
+    pl.semaphore_signal(barrier, inc=1, device_id={"groups": other}, device_id_type=pl.DeviceIdType.MESH)
+    pl.semaphore_wait(barrier, 1 + has[0].astype(jnp.int32) + has[1].astype(jnp.int32))
+
+    def place(index, half, chunk):
+        return pl.ds(pl.multiple_of(index * block + half * share + chunk * rows, rows), rows)
+
+    def along_z(side, index, distance, chunk, source):
+        return pltpu.make_async_remote_copy(
+            src_ref=source,
+            dst_ref=gathered.at[place(index, group, chunk)],
+            send_sem=z_send.at[side, distance, chunk],
+            recv_sem=z_recv.at[side, distance, chunk],
+            device_id={"train": neighbour[side]},
+            device_id_type=pl.DeviceIdType.MESH,
+        )
+
+    def along_y(side, index, half, distance, chunk):
+        return pltpu.make_async_remote_copy(
+            src_ref=gathered.at[place(index, half, chunk)],
+            dst_ref=gathered.at[place(index, half, chunk)],
+            send_sem=y_send.at[side, distance, chunk],
+            recv_sem=y_recv.at[side, distance, chunk],
+            device_id={"groups": other},
+            device_id_type=pl.DeviceIdType.MESH,
+        )
+
+    def own(chunk):
+        return own_ref.at[pl.ds(pl.multiple_of(group * share + chunk * rows, rows), rows)]
+
+    def first(chunk, _):
+        for side in range(2):
+
+            @pl.when(has[side])
+            def _(side=side):
+                along_z(side, position, 0, chunk, own(chunk)).start()
+
+        return 0
+
+    lax.fori_loop(0, chunks, first, 0)
+    load.wait()
+
+    def score(source, index, chunk):
+        columns = pl.ds(pl.multiple_of(chunk * width, width), width)
+        product_ref[pl.ds(pl.multiple_of(index * block, block), block), columns] = lax.dot_general(
+            source, train[columns, :], (((1,), (1,)), ((), ())), preferred_element_type=jnp.float32
+        )
+
+    def turn(step, _):
+        def slot(chunk, _):
+            for side in range(2):
+                index = position - 1 - step if side == 1 else position + 1 + step
+                arrives = index >= 0 if side == 1 else index < cycle
+
+                @pl.when(arrives)
+                def _(side=side, index=index):
+                    here = gathered.at[place(index, group, chunk)]
+                    along_z(side, index, step, chunk, here).wait_recv()
+
+                    @pl.when(has[side])
+                    def _():
+                        along_z(side, index, step + 1, chunk, here).start()
+
+                    along_y(side, index, group, step, chunk).start()
+
+            for side in range(2):
+                index = position - step if side == 1 else position + step
+                arrived = index >= 0 if side == 1 else index < cycle
+
+                @pl.when((step > 0) & arrived)
+                def _(side=side, index=index):
+                    @pl.when(chunk == 0)
+                    def _():
+                        def landed(piece, _):
+                            along_y(side, index, other, step - 1, piece).wait_recv()
+                            return 0
+
+                        lax.fori_loop(0, chunks, landed, 0)
+
+                    score(gathered[pl.ds(pl.multiple_of(index * block, block), block), :], index, chunk)
+
+            @pl.when(step == 0)
+            def _():
+                score(own_ref[...], position, chunk)
+
+            return 0
+
+        return lax.fori_loop(0, chunks, slot, 0)
+
+    lax.fori_loop(0, cycle, turn, 0)
+
+    def sent(step, _):
+        def piece(chunk, _):
+            for side in range(2):
+                index = position - step if side == 1 else position + step
+                held = index >= 0 if side == 1 else index < cycle
+
+                @pl.when(held & has[side])
+                def _(side=side, index=index):
+                    along_z(side, position, step, chunk, own(chunk)).wait_send()
+
+                came = index - 1 >= 0 if side == 1 else index + 1 < cycle
+
+                @pl.when(came)
+                def _(side=side):
+                    along_y(side, position, group, step, chunk).wait_send()
+
+            return 0
+
+        return lax.fori_loop(0, chunks, piece, 0)
+
+    lax.fori_loop(0, cycle, sent, 0)
+
+
+def scores_of(conditioned, train_flat):
+    cycle = lax.axis_size("train")
+    block, depth = conditioned.shape
+    slots = train_flat.shape[0]
+    chunks = max(1, min(4, block // 2 // 16))
+    return pl.pallas_call(
+        functools.partial(gather_and_score, cycle, chunks),
+        out_shape=jax.ShapeDtypeStruct((cycle * block, slots), jnp.float32),
+        in_specs=[pl.BlockSpec(memory_space=pltpu.VMEM), pl.BlockSpec(memory_space=pl.ANY)],
+        out_specs=pl.BlockSpec(memory_space=pltpu.VMEM),
+        scratch_shapes=[
+            pltpu.VMEM((cycle * block, depth), jnp.bfloat16),
+            pltpu.VMEM((slots, depth), jnp.bfloat16),
+            pltpu.SemaphoreType.DMA((2, cycle, chunks)),
+            pltpu.SemaphoreType.DMA((2, cycle, chunks)),
+            pltpu.SemaphoreType.DMA((2, cycle, chunks)),
+            pltpu.SemaphoreType.DMA((2, cycle, chunks)),
+            pltpu.SemaphoreType.DMA,
+        ],
+        compiler_params=pltpu.CompilerParams(
+            collective_id=0, has_side_effects=True, vmem_limit_bytes=48 * 1024 * 1024
+        ),
+        cost_estimate=pl.CostEstimate(flops=2 * cycle * block * slots * depth, bytes_accessed=2 * slots * depth, transcendentals=0),
+    )(conditioned, train_flat)
+
+
 def body(query_grads, train_grads, left_inverse, right_inverse, valid_rows, query_order):
-    groups = lax.axis_size("groups")
-    share = query_grads.shape[0] // groups
-    own = lax.dynamic_slice_in_dim(query_grads, lax.axis_index("groups") * share, share, 0)
-    conditioned = precondition(own, left_inverse, right_inverse).reshape(share, -1)
-    conditioned = lax.all_gather(conditioned, ("train", "groups"), axis=0, tiled=True)
-    train_flat = train_grads.reshape(train_grads.shape[0], -1)
-    product = lax.dot_general(
-        conditioned, train_flat, (((1,), (1,)), ((), ())), preferred_element_type=jnp.float32
-    )
-    live = jnp.arange(train_flat.shape[0], dtype=jnp.int32) < valid_rows[0]
-    product = jnp.where(live[None, :], product, 0.0)
+    conditioned = precondition(query_grads, left_inverse, right_inverse).reshape(query_grads.shape[0], -1)
+    product = scores_of(conditioned, train_grads.reshape(train_grads.shape[0], -1))
     ordered = jnp.take(product, query_order, axis=0)
-    return summed_over_layers(ordered)
+    scores = summed_over_layers(ordered)
+    live = jnp.arange(scores.shape[1], dtype=jnp.int32) < valid_rows[0]
+    return jnp.where(live[None, :], scores, 0.0)
 
 
 def solution(mesh):

time: 207 us -> 140 us (0.68)
  waiting for transfers between devices: 145 us -> 16 us
  Pallas kernels: 0 us -> 86.8 us
  between operations: 14.2 us -> 0.82 us
  matrix products: 20.8 us -> 9.48 us
    all_gather x1 -> x0, waiting for transfers between devices: 128 us -> none  [body(): lax.all_gather(conditioned, ('train', 'groups'), axis=0, tiled=True)]
    pallas_call x0 -> x1, Pallas kernels: none -> 86.8 us  [scores_of(): pl.pallas_call(functools.partial(gather_and_score, cycle, chunks), out_sh...]
    dot_general x1 -> x0, matrix products: 15.2 us -> none  [body(): lax.dot_general(conditioned, train_flat, (((1,), (1,)), ((), ())), prefer...]
    convert_element_type x0 -> x1, local copies, waits for them, and re-layouts: none -> 2.91 us  [precondition(): matrix.reshape(row_count, layer_count, order_in * order_out)]
    dot_general x1, matrix products: 4.25 us -> 6.79 us  [precondition(): jnp.einsum('rlac,lcd->rlad', matrix, right_factor, precision=lax.Precisio...]
    reshape x1 -> x0, other arithmetic: 2.38 us -> none  [summed_over_layers(): return blocks.reshape(-1, columns)]
    unnamed x13 -> x7, local copies, waits for them, and re-layouts: 6.47 us -> 5.21 us
  transfers between devices with their start and end apart: 3 -> 2, of which waited for: 3 -> 2; matrix products, arithmetic and copies ran while one was open for 0% -> 0% of each run, Pallas kernels for 0% -> 0%
where the time goes in v2:
time: 140 us; the launch traced here: 139 us
  Pallas kernels  86.8 us (62%)
  local copies, waits for them, and re-layouts  17.1 us (12%)
  waiting for transfers between devices  16 us (11%)
  matrix products  9.48 us (7%)
  other arithmetic  7.66 us (5%)
  starting transfers between devices  1.62 us (1%)
    pallas_call x1, Pallas kernels, scores_of(): pl.pallas_call(functools.partial(gather_and_score, cycle, chunks), out_sh...  86.8 us
    ppermute x2, waiting for transfers between devices, summed_over_layers(): taken = lax.ppermute(given, 'layer', route)  16 us
    gather x1, local copies, waits for them, and re-layouts, body(): ordered = jnp.take(product, query_order, axis=0)  8.63 us
    dot_general x1, matrix products, precondition(): jnp.einsum('rlac,lcd->rlad', matrix, right_factor, precision=lax.Precisio...  6.79 us
    unnamed x7, local copies, waits for them, and re-layouts  5.21 us
    convert_element_type x1, local copies, waits for them, and re-layouts, precondition(): matrix.reshape(row_count, layer_count, order_in * order_out)  2.91 us
  transfers between devices with their start and end apart: 2, of which 2 were waited for; matrix products, arithmetic and copies ran while one was open for 0% of the time, Pallas kernels for 0%

profile of v2, /device:TPU:0, one launch (start us, length us, event | category | flops | bytes accessed | tf_op | source)
XLA Modules:
  0.0 139.5 jit_solution(9309464815674793750)
XLA Ops:
  0.0 0.0 copy-start
  0.0 0.7 compare_and_fusion
  0.7 0.7 fusion.8
  1.4 3.3 %copy.11 = bf16[256,1,4096]{0,2,1:T(8,128)(2,1)S(1)} copy(bf16[256,1,4096]{2,0,1:T(8,128)(2,1)} %param.6) | data formatting | bytes 4194304 | tf_op args[0]
  4.7 0.0 copy-start.2
  4.7 0.0 copy-done
  4.7 2.7 %convolution_bitcast_fusion = f32[256,64,64]{0,1,2:T(8,128)S(1)} fusion(bf16[256,64,64]{0,2,1:T(8,128)(2,1)S(1)} %bitcast.35, f32[1,64,64]{2,1,0:T(8,128)S(1)} %copy-done), kind=kOutput, calls=%fused_computation.3 | convolution fusion | flops 805306368 | bytes 6307840 | tf_op jit(solution)/shard_map/lab,rlbc->rlac/dot_general | solution.py:17
  7.4 0.0 copy-done.2
  7.4 6.8 %fusion.3 = bf16[256,64,64]{0,2,1:T(8,128)(2,1)} fusion(f32[256,64,64]{0,1,2:T(8,128)S(1)} %convolution_bitcast_fusion, f32[1,64,64]{2,1,0:T(8,128)S(1)} %copy-done.2), kind=kOutput, calls=%fused_computation.8 | convolution fusion | flops 806354944 | bytes 6307840 | tf_op jit(solution)/shard_map/rlac,lcd->rlad/dot_general | solution.py:18
  14.2 2.9 %copy.15.own_ref = bf16[256,4096]{1,0:T(8,128)(2,1)S(1)} copy(bf16[256,4096]{0,1:T(8,128)(2,1)} %bitcast.34) | data formatting | bytes 4194304 | tf_op jit(solution)/shard_map/convert_element_type | solution.py:19
  17.1 86.8 %shard_map.64 = f32[1024,1024]{1,0:T(8,128)} custom-call(bf16[256,4096]{1,0:T(8,128)(2,1)S(1)} %copy.15.own_ref, bf16[1024,4096]{1,0:T(8,128)(2,1)} %bitcast.36), custom_call_target="tpu_custom_call" | custom-call | flops 8589934592 | bytes 8388608 | tf_op jit(solution)/shard_map/pallas_call | solution.py:181
  103.9 8.6 %gather_fusion = f32[1024,1024]{1,0:T(8,128)} fusion(f32[1024,1024]{1,0:T(8,128)} %shard_map.64, s32[1024]{0:T(1024)S(1)} %fusion.8), kind=kCustom, calls=%fused_computation | custom fusion | bytes 8392704 | tf_op jit(solution)/shard_map/jit(_take)/gather | solution.py:205
  112.6 2.5 %broadcast_select_fusion = f32[2,2,256,1024]{3,2,1,0:T(8,128)S(1)} fusion(f32[2,2,256,1024]{3,2,1,0:T(8,128)} %bitcast.33, pred[2,2,256]{2,1,0:T(4,128)(4,1)S(1)} %broadcast_in_dim.28), kind=kLoop, calls=%fused_computation.7 | loop fusion | flops 1048576 | bytes 8389632 | tf_op jit(solution)/shard_map/jit(_take)/select_n | solution.py:205
  115.1 0.0 copy-start.1
  115.1 1.9 %copy-done.1 = f32[2,2,256,1024]{3,2,1,0:T(8,128)} copy-done((f32[2,2,256,1024]{3,2,1,0:T(8,128)}, f32[2,2,256,1024]{3,2,1,0:T(8,128)S(1)}, u32[]{:S(2)}) %copy-start.1) | copy-done | bytes 4194328
  117.0 0.2 dynamic-slice_bitcast_fusion
  117.3 0.1 collective-permute-start
  117.4 4.2 %collective-permute-done = f32[2,256,1024]{2,1,0:T(8,128)} collective-permute-done((f32[2,256,1024]{2,1,0:T(8,128)S(1)}, f32[2,256,1024]{2,1,0:T(8,128)}, u32[]{:S(2)}, u32[]{:S(2)}) %collective-permute-start) | collective-permute-done | bytes 2097184 | tf_op jit(solution)/shard_map/ppermute | solution.py:37
  121.6 2.6 %bitcast_add_fusion = f32[2,256,1024]{2,1,0:T(8,128)S(1)} fusion(f32[2,256,1024]{2,1,0:T(8,128)} %collective-permute-done, f32[2,2,256,1024]{3,2,1,0:T(8,128)} %copy-done.1, s32[]{:T(128)S(6)} %select_n.47), kind=kLoop, calls=%fused_computation.4 | loop fusion | flops 524288 | bytes 6291460 | tf_op jit(solution)/shard_map/add | solution.py:38
  124.3 0.1 dynamic-slice_convert_fusion
  124.4 1.6 %collective-permute-start.1 = (bf16[1,256,1024]{2,1,0:T(8,128)(2,1)S(1)}, bf16[1,256,1024]{2,1,0:T(8,128)(2,1)S(1)}, u32[]{:S(2)}, u32[]{:S(2)}) collective-permute-start(bf16[1,256,1024]{2,1,0:T(8,128)(2,1)S(1)} %dynamic-slice_convert_fusion), channel_id=1, source_target_pairs={{0,2},{1,3},{2,0},{3,1},{4,6},{5,7},{6,4},{7,5},{8,10},{9,11},{10,... | collective-permute-start | bytes 1572872 | tf_op jit(solution)/shard_map/ppermute | solution.py:37
  126.6 11.8 %collective-permute-done.1 = bf16[1,256,1024]{2,1,0:T(8,128)(2,1)S(1)} collective-permute-done((bf16[1,256,1024]{2,1,0:T(8,128)(2,1)S(1)}, bf16[1,256,1024]{2,1,0:T(8,128)(2,1)S(1)}, u32[]{:S(2)}, u32[]{:S(2)}) %collective-permute-start.1) | collective-permute-done | bytes 524320 | tf_op jit(solution)/shard_map/ppermute | solution.py:37
  138.4 1.1 bitcast_select_fusion
  (2 shorter events, 0.0 us)
Async XLA Ops:
  0.0 4.7 %copy-start = (f32[1,64,64]{2,1,0:T(8,128)S(1)}, f32[1,64,64]{2,1,0:T(8,128)}, u32[]{:S(2)}) copy-start(f32[1,64,64]{2,1,0:T(8,128)} %param.8) | copy-start | bytes 49156
  4.7 2.7 %copy-start.2 = (f32[1,64,64]{2,1,0:T(8,128)S(1)}, f32[1,64,64]{2,1,0:T(8,128)}, u32[]{:S(2)}) copy-start(f32[1,64,64]{2,1,0:T(8,128)} %param.9) | copy-start | bytes 49156
  115.1 1.9 %copy-start.1 = (f32[2,2,256,1024]{3,2,1,0:T(8,128)}, f32[2,2,256,1024]{3,2,1,0:T(8,128)S(1)}, u32[]{:S(2)}) copy-start(f32[2,2,256,1024]{3,2,1,0:T(8,128)S(1)} %broadcast_select_fusion) | copy-start | bytes 12582916
  117.3 4.4 %collective-permute-start = (f32[2,256,1024]{2,1,0:T(8,128)S(1)}, f32[2,256,1024]{2,1,0:T(8,128)}, u32[]{:S(2)}, u32[]{:S(2)}) collective-permute-start(f32[2,256,1024]{2,1,0:T(8,128)S(1)} %dynamic-slice_bitcast_fusion), channel_id=1, source_target_pairs={{0,1},{1,0},{2,3},{3,2},{4,5},{5,4},{6,7},{7,6},{8,9},{9,8},{10,11... | collective-permute-start | bytes 6291464 | tf_op jit(solution)/shard_map/ppermute | solution.py:37
  124.4 14.0 %collective-permute-start.1 = (bf16[1,256,1024]{2,1,0:T(8,128)(2,1)S(1)}, bf16[1,256,1024]{2,1,0:T(8,128)(2,1)S(1)}, u32[]{:S(2)}, u32[]{:S(2)}) collective-permute-start(bf16[1,256,1024]{2,1,0:T(8,128)(2,1)S(1)} %dynamic-slice_convert_fusion), channel_id=1, source_target_pairs={{0,2},{1,3},{2,0},{3,1},{4,6},{5,7},{6,4},{7,5},{8,10},{9,11},{10,... | collective-permute-start | bytes 1572872 | tf_op jit(solution)/shard_map/ppermute | solution.py:37

commit v3 on v2

v3 whole, which is shorter than its diff:
```python
import functools

import jax
import jax.numpy as jnp
from jax import lax
from jax.experimental import pallas as pl
from jax.experimental.pallas import tpu as pltpu
from jax.sharding import PartitionSpec as P


def precondition(gradients, left_factor, right_factor):
    row_count = gradients.shape[0]
    layer_count = left_factor.shape[0]
    order_in = left_factor.shape[-1]
    order_out = right_factor.shape[-1]
    matrix = gradients.astype(jnp.float32).reshape(row_count, layer_count, order_in, order_out)
    matrix = jnp.einsum("lab,rlbc->rlac", left_factor, matrix, precision=lax.Precision.HIGHEST)
    matrix = jnp.einsum("rlac,lcd->rlad", matrix, right_factor, precision=lax.Precision.HIGHEST)
    return matrix.reshape(row_count, layer_count, order_in * order_out).astype(jnp.bfloat16)


MESH = pl.DeviceIdType.MESH


def gather_and_score(cycle, chunks, stages, own_ref, train_ref, order_ref, out_ref, gathered, train, give, taken, total, x_out, x_in, handed,
                     z_send, z_recv, y_send, y_recv, c_send, c_recv, x_send, x_recv, local_sem, last_sem):
    position = lax.axis_index("train")
    group = lax.axis_index("groups")
    layer = lax.axis_index("layer")
    core = layer % 2
    block = own_ref.shape[0]
    share = block // 2
    rows = share // chunks
    parts = chunks // 2
    width = train.shape[0] // chunks
    half = parts * width
    load = pltpu.make_async_copy(train_ref, train, local_sem.at[0])
    load.start()

    def block_of(index):
        return pl.ds(pl.multiple_of(index * block, block), block)

    move = pltpu.make_async_copy(own_ref, gathered.at[block_of(position)], local_sem.at[1])
    move.start()

    has = (position > 0, position < cycle - 1)
    neighbour = ((position + cycle - 1) % cycle, (position + 1) % cycle)
    other = 1 - group
    sibling = layer + 1 - 2 * core
    partners = [layer + bit * (1 - 2 * ((layer // bit) % 2)) for bit in (2 << k for k in range(stages))]
    barrier = pltpu.get_barrier_semaphore()
    for side in range(2):

        @pl.when(has[side])
        def _(side=side):
            pl.semaphore_signal(barrier, inc=1, device_id={"train": neighbour[side]}, device_id_type=MESH)

    pl.semaphore_signal(barrier, inc=1, device_id={"groups": other}, device_id_type=MESH)
    for partner in [sibling] + partners:
        pl.semaphore_signal(barrier, inc=1, device_id={"layer": partner}, device_id_type=MESH)
    pl.semaphore_wait(barrier, 2 + stages + has[0].astype(jnp.int32) + has[1].astype(jnp.int32))

    def place(index, side, chunk):
        return pl.ds(pl.multiple_of(index * block + side * share + chunk * rows, rows), rows)

    def along_z(side, index, distance, chunk, source):
        return pltpu.make_async_remote_copy(
            src_ref=source,
            dst_ref=gathered.at[place(index, group, chunk)],
            send_sem=z_send.at[side, distance, chunk],
            recv_sem=z_recv.at[side, distance, chunk],
            device_id={"train": neighbour[side]},
            device_id_type=MESH,
        )

    def along_y(side, index, which, distance, chunk):
        return pltpu.make_async_remote_copy(
            src_ref=gathered.at[place(index, which, chunk)],
            dst_ref=gathered.at[place(index, which, chunk)],
            send_sem=y_send.at[side, distance, chunk],
            recv_sem=y_recv.at[side, distance, chunk],
            device_id={"groups": other},
            device_id_type=MESH,
        )

    def part_of(part):
        return pl.ds(pl.multiple_of(part * width, width), width)

    def to_core(side, index, distance, part):
        return pltpu.make_async_remote_copy(
            src_ref=give.at[block_of(index), part_of(part)],
            dst_ref=taken.at[block_of(index), part_of(part)],
            send_sem=c_send.at[side, distance, part],
            recv_sem=c_recv.at[side, distance, part],
            device_id={"layer": sibling},
            device_id_type=MESH,
        )

    def along_x(stage, side, index, distance, part):
        return pltpu.make_async_remote_copy(
            src_ref=x_out.at[stage, block_of(index), part_of(part)],
            dst_ref=x_in.at[stage, block_of(index), part_of(part)],
            send_sem=x_send.at[stage, side, distance, part],
            recv_sem=x_recv.at[stage, side, distance, part],
            device_id={"layer": partners[stage]},
            device_id_type=MESH,
        )

    def own(chunk):
        return own_ref.at[pl.ds(pl.multiple_of(group * share + chunk * rows, rows), rows)]

    def first(chunk, _):
        for side in range(2):

            @pl.when(has[side])
            def _(side=side):
                along_z(side, position, 0, chunk, own(chunk)).start()

        return 0

    lax.fori_loop(0, chunks, first, 0)
    move.wait()
    load.wait()

    def at(side, distance):
        if side == 1:
            return position - distance, position - distance >= 0
        return position + distance, (position + distance < cycle) & (distance > 0)

    def absorb(side, index, distance, part):
        for stage in range(stages):
            along_x(stage, side, index, distance, part).wait_recv()
            sums = total[block_of(index), part_of(part)] + x_in[stage, block_of(index), part_of(part)].astype(jnp.float32)
            total[block_of(index), part_of(part)] = sums
            if stage + 1 < stages:
                x_out[stage + 1, block_of(index), part_of(part)] = sums.astype(jnp.bfloat16)
                along_x(stage + 1, side, index, distance, part).start()

    def turn(step, _):
        def slot(chunk, _):
            for side in range(2):
                index = position - 1 - step if side == 1 else position + 1 + step
                arrives = index >= 0 if side == 1 else index < cycle

                @pl.when(arrives)
                def _(side=side, index=index):
                    here = gathered.at[place(index, group, chunk)]
                    along_z(side, index, step, chunk, here).wait_recv()

                    @pl.when(has[side])
                    def _():
                        along_z(side, index, step + 1, chunk, here).start()

                    along_y(side, index, group, step, chunk).start()

            for side in range(2):
                index, there = at(side, step - 1)

                @pl.when((step > 0) & there & (chunk < parts))
                def _(side=side, index=index):
                    absorb(side, index, step - 1, chunk)

            mine = chunk // parts
            part = chunk - mine * parts
            columns = pl.ds(
                pl.multiple_of(((1 - core) * (1 - mine) + core * mine) * half + part * width, width), width
            )
            for side in range(2):
                index, there = at(side, step)

                @pl.when(there)
                def _(side=side, index=index):
                    @pl.when((chunk == 0) & (step > 0))
                    def _():
                        def landed(piece, _):
                            along_y(side, index, other, step - 1, piece).wait_recv()
                            return 0

                        lax.fori_loop(0, chunks, landed, 0)

                    product = lax.dot_general(
                        gathered[block_of(index), :],
                        train[columns, :],
                        (((1,), (1,)), ((), ())),
                        preferred_element_type=jnp.float32,
                    )

                    @pl.when(mine == 0)
                    def _():
                        give[block_of(index), part_of(part)] = product
                        to_core(side, index, step, part).start()

                    @pl.when(mine == 1)
                    def _():
                        to_core(side, index, step, part).wait_recv()
                        sums = product + taken[block_of(index), part_of(part)]
                        total[block_of(index), part_of(part)] = sums
                        x_out[0, block_of(index), part_of(part)] = sums.astype(jnp.bfloat16)
                        along_x(0, side, index, step, part).start()

            return 0

        return lax.fori_loop(0, chunks, slot, 0)

    lax.fori_loop(0, cycle, turn, 0)

    for side in range(2):
        index, there = at(side, cycle - 1)

        @pl.when(there)
        def _(side=side, index=index):
            def rest(part, _):
                absorb(side, index, cycle - 1, part)
                return 0

            lax.fori_loop(0, parts, rest, 0)

    count = out_ref.shape[0]
    lanes = pl.ds(pl.multiple_of(core * half, half), half)
    step_rows = 8

    def pick(owner, target):
        def eight(i, _):
            picked = [
                total[pl.ds(order_ref[owner * count + i * step_rows + k], 1), :] for k in range(step_rows)
            ]
            target[pl.ds(pl.multiple_of(i * step_rows, step_rows), step_rows), :] = jnp.concatenate(picked, axis=0)
            return 0

        lax.fori_loop(0, count // step_rows, eight, 0)

    pick(sibling, handed)
    last = pltpu.make_async_remote_copy(
        src_ref=handed,
        dst_ref=out_ref.at[:, lanes],
        send_sem=last_sem.at[0],
        recv_sem=last_sem.at[1],
        device_id={"layer": sibling},
        device_id_type=MESH,
    )
    last.start()
    pick(layer, out_ref.at[:, lanes])

    def sent(step, _):
        def piece(chunk, _):
            for side in range(2):
                index = position - step if side == 1 else position + step
                held = index >= 0 if side == 1 else index < cycle

                @pl.when(held & has[side])
                def _(side=side):
                    along_z(side, position, step, chunk, own(chunk)).wait_send()

                came = index - 1 >= 0 if side == 1 else index + 1 < cycle

                @pl.when(came)
                def _(side=side):
                    along_y(side, position, group, step, chunk).wait_send()

                _, there = at(side, step)

                @pl.when(there & (chunk < parts))
                def _(side=side):
                    to_core(side, position, step, chunk).wait_send()
                    for stage in range(stages):
                        along_x(stage, side, position, step, chunk).wait_send()

            return 0

        return lax.fori_loop(0, chunks, piece, 0)

    lax.fori_loop(0, cycle, sent, 0)
    last.wait()


def scores_of(conditioned, train_flat, query_order):
    cycle = lax.axis_size("train")
    layers = lax.axis_size("layer")
    stages = (layers // 2).bit_length() - 1
    block, depth = conditioned.shape
    slots = train_flat.shape[0]
    queries = cycle * block
    count = queries // layers
    chunks = min(4, block // 2 // 16)
    parts = chunks // 2
    dma = pltpu.SemaphoreType.DMA
    return pl.pallas_call(
        functools.partial(gather_and_score, cycle, chunks, stages),
        out_shape=jax.ShapeDtypeStruct((count, slots), jnp.float32),
        in_specs=[
            pl.BlockSpec(memory_space=pltpu.VMEM),
            pl.BlockSpec(memory_space=pl.ANY),
            pl.BlockSpec(memory_space=pltpu.SMEM),
        ],
        out_specs=pl.BlockSpec(memory_space=pltpu.VMEM),
        scratch_shapes=[
            pltpu.VMEM((queries, depth), jnp.bfloat16),
            pltpu.VMEM((slots, depth), jnp.bfloat16),
            pltpu.VMEM((queries, slots // 2), jnp.float32),
            pltpu.VMEM((queries, slots // 2), jnp.float32),
            pltpu.VMEM((queries, slots // 2), jnp.float32),
            pltpu.VMEM((stages, queries, slots // 2), jnp.bfloat16),
            pltpu.VMEM((stages, queries, slots // 2), jnp.bfloat16),
            pltpu.VMEM((count, slots // 2), jnp.float32),
            dma((2, cycle, chunks)),
            dma((2, cycle, chunks)),
            dma((2, cycle, chunks)),
            dma((2, cycle, chunks)),
            dma((2, cycle, parts)),
            dma((2, cycle, parts)),
            dma((stages, 2, cycle, parts)),
            dma((stages, 2, cycle, parts)),
            dma((2,)),
            dma((2,)),
        ],
        compiler_params=pltpu.CompilerParams(
            collective_id=0, has_side_effects=True, vmem_limit_bytes=50 * 1024 * 1024
        ),
        cost_estimate=pl.CostEstimate(
            flops=2 * queries * slots * depth, bytes_accessed=2 * slots * depth, transcendentals=0
        ),
    )(conditioned, train_flat, query_order)


def body(query_grads, train_grads, left_inverse, right_inverse, valid_rows, query_order):
    conditioned = precondition(query_grads, left_inverse, right_inverse).reshape(query_grads.shape[0], -1)
    scores = scores_of(conditioned, train_grads.reshape(train_grads.shape[0], -1), query_order)
    live = jnp.arange(scores.shape[1], dtype=jnp.int32) < valid_rows[0]
    return jnp.where(live[None, :], scores, 0.0)


def solution(mesh):
    return jax.shard_map(
        body,
        mesh=mesh,
        in_specs=(
            P("train", "layer", None),
            P(("groups", "train"), "layer", None),
            P("layer", None, None),
            P("layer", None, None),
            P(("groups", "train")),
            P(),
        ),
        out_specs=P("layer", ("groups", "train")),
        check_vma=False,
    )
```

time: 140 us -> 115 us (0.82)
  waiting for transfers between devices: 16 us -> 0 us
  local copies, waits for them, and re-layouts: 17.1 us -> 6.21 us
  Pallas kernels: 86.8 us -> 96.9 us
  other arithmetic: 7.66 us -> 1.09 us
  starting transfers between devices: 1.62 us -> 0 us
    ppermute x2 -> x0, waiting for transfers between devices: 16 us -> none  [summed_over_layers(): taken = lax.ppermute(given, 'layer', route)]
    pallas_call x1, Pallas kernels: 86.8 us -> 96.9 us  [scores_of(): pl.pallas_call(functools.partial(gather_and_score, cycle, chunks, stages)...]
    gather x1 -> x0, local copies, waits for them, and re-layouts: 8.63 us -> none  [body(): ordered = jnp.take(product, query_order, axis=0)]
    add x1 -> x0, other arithmetic: 2.61 us -> none  [summed_over_layers(): blocks = kept + taken.astype(jnp.float32)]
    select_n x1 -> x0, other arithmetic: 2.54 us -> none  [body(): ordered = jnp.take(product, query_order, axis=0)]
    unnamed x7, local copies, waits for them, and re-layouts: 5.21 us -> 3.29 us
    ppermute x2 -> x0, starting transfers between devices: 1.62 us -> none  [summed_over_layers(): taken = lax.ppermute(given, 'layer', route)]
  transfers between devices with their start and end apart: 2 -> 0, of which waited for: 2 -> 0; matrix products, arithmetic and copies ran while one was open for 0% -> 0% of each run, Pallas kernels for 0% -> 0%
where the time goes in v3:
time: 115 us; the launch traced here: 114 us
  Pallas kernels  96.9 us (84%)
  matrix products  9.48 us (8%)
  local copies, waits for them, and re-layouts  6.21 us (5%)
    pallas_call x1, Pallas kernels, scores_of(): pl.pallas_call(functools.partial(gather_and_score, cycle, chunks, stages)...  96.9 us
    dot_general x1, matrix products, precondition(): jnp.einsum('rlac,lcd->rlad', matrix, right_factor, precision=lax.Precisio...  6.79 us
    unnamed x7, local copies, waits for them, and re-layouts  3.29 us
    convert_element_type x1, local copies, waits for them, and re-layouts, precondition(): matrix.reshape(row_count, layer_count, order_in * order_out)  2.92 us
    dot_general x1, matrix products, precondition(): jnp.einsum('lab,rlbc->rlac', left_factor, matrix, precision=lax.Precision...  2.69 us

profile of v3, /device:TPU:0, one launch (start us, length us, event | category | flops | bytes accessed | tf_op | source)
XLA Modules:
  0.0 114.4 jit_solution(8418699725835898246)
XLA Ops:
  0.0 0.0 copy-start
  0.0 3.3 %copy.11 = bf16[256,1,4096]{0,2,1:T(8,128)(2,1)S(1)} copy(bf16[256,1,4096]{2,0,1:T(8,128)(2,1)} %param.6) | data formatting | bytes 4194304 | tf_op args[0]
  3.3 0.0 copy-done
  3.3 0.0 copy-start.2
  3.3 2.7 %convolution_bitcast_fusion = f32[256,64,64]{0,1,2:T(8,128)S(1)} fusion(bf16[256,64,64]{0,2,1:T(8,128)(2,1)S(1)} %bitcast.27, f32[1,64,64]{2,1,0:T(8,128)S(1)} %copy-done), kind=kOutput, calls=%fused_computation.2 | convolution fusion | flops 805306368 | bytes 6307840 | tf_op jit(solution)/shard_map/lab,rlbc->rlac/dot_general | solution.py:17
  6.0 0.0 copy-done.2
  6.0 6.8 %fusion.3 = bf16[256,64,64]{0,2,1:T(8,128)(2,1)} fusion(f32[256,64,64]{0,1,2:T(8,128)S(1)} %convolution_bitcast_fusion, f32[1,64,64]{2,1,0:T(8,128)S(1)} %copy-done.2), kind=kOutput, calls=%fused_computation.4 | convolution fusion | flops 806354944 | bytes 6307840 | tf_op jit(solution)/shard_map/rlac,lcd->rlad/dot_general | solution.py:18
  12.8 0.0 copy-start.1
  12.8 2.9 %copy.15.own_ref = bf16[256,4096]{1,0:T(8,128)(2,1)S(1)} copy(bf16[256,4096]{0,1:T(8,128)(2,1)} %bitcast.26) | data formatting | bytes 4194304 | tf_op jit(solution)/shard_map/convert_element_type | solution.py:19
  15.7 0.0 copy-done.1
  15.7 96.9 %shard_map.64 = f32[256,1024]{1,0:T(8,128)S(1)} custom-call(bf16[256,4096]{1,0:T(8,128)(2,1)S(1)} %copy.15.own_ref, bf16[1024,4096]{1,0:T(8,128)(2,1)} %bitcast.28, s32[1024]{0:T(1024)S(1)} %copy-done.1), custom_call_target="tpu_custom_call" | custom-call | flops 8589934592 | bytes 8388608 | tf_op jit(solution)/shard_map/pallas_call | solution.py:287
  113.3 1.1 broadcast_select_fusion
  (1 shorter events, 0.0 us)
Async XLA Ops:
  0.0 3.3 %copy-start = (f32[1,64,64]{2,1,0:T(8,128)S(1)}, f32[1,64,64]{2,1,0:T(8,128)}, u32[]{:S(2)}) copy-start(f32[1,64,64]{2,1,0:T(8,128)} %param.8) | copy-start | bytes 49156
  3.3 2.7 %copy-start.2 = (f32[1,64,64]{2,1,0:T(8,128)S(1)}, f32[1,64,64]{2,1,0:T(8,128)}, u32[]{:S(2)}) copy-start(f32[1,64,64]{2,1,0:T(8,128)} %param.9) | copy-start | bytes 49156
  12.8 2.9 %copy-start.1 = (s32[1024]{0:T(1024)S(1)}, s32[1024]{0:T(1024)}, u32[]{:S(2)}) copy-start(s32[1024]{0:T(1024)} %order_ref.1) | copy-start | bytes 12292

commit v4 on v3

--- a/solution.py
+++ b/solution.py
@@ -14,15 +14,15 @@
     order_in = left_factor.shape[-1]
     order_out = right_factor.shape[-1]
     matrix = gradients.astype(jnp.float32).reshape(row_count, layer_count, order_in, order_out)
-    matrix = jnp.einsum("lab,rlbc->rlac", left_factor, matrix, precision=lax.Precision.HIGHEST)
-    matrix = jnp.einsum("rlac,lcd->rlad", matrix, right_factor, precision=lax.Precision.HIGHEST)
+    matrix = jnp.einsum("lab,rlbc->rlac", left_factor, matrix, precision=lax.Precision.HIGH)
+    matrix = jnp.einsum("rlac,lcd->rlad", matrix, right_factor, precision=lax.Precision.HIGH)
     return matrix.reshape(row_count, layer_count, order_in * order_out).astype(jnp.bfloat16)
 
 
 MESH = pl.DeviceIdType.MESH
 
 
-def gather_and_score(cycle, chunks, stages, own_ref, train_ref, order_ref, out_ref, gathered, train, give, taken, total, x_out, x_in, handed,
+def gather_and_score(cycle, chunks, pieces, stages, own_ref, train_ref, order_ref, out_ref, gathered, train, give, taken, total, x_out, x_in, handed,
                      z_send, z_recv, y_send, y_recv, c_send, c_recv, x_send, x_recv, local_sem, last_sem):
     position = lax.axis_index("train")
     group = lax.axis_index("groups")
@@ -31,8 +31,9 @@
     block = own_ref.shape[0]
     share = block // 2
     rows = share // chunks
-    parts = chunks // 2
-    width = train.shape[0] // chunks
+    parts = pieces // 2
+    width = train.shape[0] // pieces
+    pace = chunks // pieces
     half = parts * width
     load = pltpu.make_async_copy(train_ref, train, local_sem.at[0])
     load.start()
@@ -153,27 +154,29 @@
 
                     along_y(side, index, group, step, chunk).start()
 
+            piece = chunk // pace
+            due = chunk % pace == 0
             for side in range(2):
                 index, there = at(side, step - 1)
 
-                @pl.when((step > 0) & there & (chunk < parts))
+                @pl.when((step > 0) & there & due & (piece < parts))
                 def _(side=side, index=index):
-                    absorb(side, index, step - 1, chunk)
-
-            mine = chunk // parts
-            part = chunk - mine * parts
+                    absorb(side, index, step - 1, piece)
+
+            mine = piece // parts
+            part = piece - mine * parts
             columns = pl.ds(
                 pl.multiple_of(((1 - core) * (1 - mine) + core * mine) * half + part * width, width), width
             )
             for side in range(2):
                 index, there = at(side, step)
 
-                @pl.when(there)
+                @pl.when(there & due)
                 def _(side=side, index=index):
                     @pl.when((chunk == 0) & (step > 0))
                     def _():
-                        def landed(piece, _):
-                            along_y(side, index, other, step - 1, piece).wait_recv()
+                        def landed(k, _):
+                            along_y(side, index, other, step - 1, k).wait_recv()
                             return 0
 
                         lax.fori_loop(0, chunks, landed, 0)
@@ -281,11 +284,12 @@
     slots = train_flat.shape[0]
     queries = cycle * block
     count = queries // layers
-    chunks = min(4, block // 2 // 16)
-    parts = chunks // 2
+    chunks = min(8, block // 2 // 16)
+    pieces = min(4, chunks)
+    parts = pieces // 2
     dma = pltpu.SemaphoreType.DMA
     return pl.pallas_call(
-        functools.partial(gather_and_score, cycle, chunks, stages),
+        functools.partial(gather_and_score, cycle, chunks, pieces, stages),
         out_shape=jax.ShapeDtypeStruct((count, slots), jnp.float32),
         in_specs=[
             pl.BlockSpec(memory_space=pltpu.VMEM),

time: 115 us -> 111 us (0.965)
  Pallas kernels: 96.9 us -> 94.7 us
  matrix products: 9.48 us -> 8 us
    pallas_call x1, Pallas kernels: 96.9 us -> 94.7 us  [scores_of(): pl.pallas_call(functools.partial(gather_and_score, cycle, chunks, pieces,...]
where the time goes in v4:
time: 111 us
  Pallas kernels  94.7 us (85%)
  matrix products  8 us (7%)
  local copies, waits for them, and re-layouts  6.21 us (6%)
    pallas_call x1, Pallas kernels, scores_of(): pl.pallas_call(functools.partial(gather_and_score, cycle, chunks, pieces,...  94.7 us
    dot_general x1, matrix products, precondition(): jnp.einsum('rlac,lcd->rlad', matrix, right_factor, precision=lax.Precisio...  5.64 us
    unnamed x7, local copies, waits for them, and re-layouts  3.29 us
    convert_element_type x1, local copies, waits for them, and re-layouts, precondition(): matrix.reshape(row_count, layer_count, order_in * order_out)  2.92 us
    dot_general x1, matrix products, precondition(): jnp.einsum('lab,rlbc->rlac', left_factor, matrix, precision=lax.Precision...  2.35 us

profile of v4, /device:TPU:0, one launch (start us, length us, event | category | flops | bytes accessed | tf_op | source)
XLA Modules:
  0.0 110.7 jit_solution(18410665216453325155)
XLA Ops:
  0.0 0.0 copy-start
  0.0 3.3 %copy.11 = bf16[256,1,4096]{0,2,1:T(8,128)(2,1)S(1)} copy(bf16[256,1,4096]{2,0,1:T(8,128)(2,1)} %param.6) | data formatting | bytes 4194304 | tf_op args[0]
  3.3 0.0 copy-done
  3.3 0.0 copy-start.2
  3.3 2.4 %convolution_bitcast_fusion = f32[256,64,64]{0,1,2:T(8,128)S(1)} fusion(bf16[256,64,64]{0,2,1:T(8,128)(2,1)S(1)} %bitcast.27, f32[1,64,64]{2,1,0:T(8,128)S(1)} %copy-done), kind=kOutput, calls=%fused_computation.2 | convolution fusion | flops 402653184 | bytes 6307840 | tf_op jit(solution)/shard_map/lab,rlbc->rlac/dot_general | solution.py:17
  5.7 0.0 copy-done.2
  5.7 5.6 %fusion.3 = bf16[256,64,64]{0,2,1:T(8,128)(2,1)} fusion(f32[256,64,64]{0,1,2:T(8,128)S(1)} %convolution_bitcast_fusion, f32[1,64,64]{2,1,0:T(8,128)S(1)} %copy-done.2), kind=kOutput, calls=%fused_computation.4 | convolution fusion | flops 403701760 | bytes 6307840 | tf_op jit(solution)/shard_map/rlac,lcd->rlad/dot_general | solution.py:18
  11.3 0.0 copy-start.1
  11.3 2.9 %copy.15.own_ref = bf16[256,4096]{1,0:T(8,128)(2,1)S(1)} copy(bf16[256,4096]{0,1:T(8,128)(2,1)} %bitcast.26) | data formatting | bytes 4194304 | tf_op jit(solution)/shard_map/convert_element_type | solution.py:19
  14.3 0.0 copy-done.1
  14.3 94.7 %shard_map.64 = f32[256,1024]{1,0:T(8,128)S(1)} custom-call(bf16[256,4096]{1,0:T(8,128)(2,1)S(1)} %copy.15.own_ref, bf16[1024,4096]{1,0:T(8,128)(2,1)} %bitcast.28, s32[1024]{0:T(1024)S(1)} %copy-done.1), custom_call_target="tpu_custom_call" | custom-call | flops 8589934592 | bytes 8388608 | tf_op jit(solution)/shard_map/pallas_call | solution.py:291
  109.6 1.1 broadcast_select_fusion
  (1 shorter events, 0.0 us)
Async XLA Ops:
  0.0 3.3 %copy-start = (f32[1,64,64]{2,1,0:T(8,128)S(1)}, f32[1,64,64]{2,1,0:T(8,128)}, u32[]{:S(2)}) copy-start(f32[1,64,64]{2,1,0:T(8,128)} %param.8) | copy-start | bytes 49156
  3.3 2.4 %copy-start.2 = (f32[1,64,64]{2,1,0:T(8,128)S(1)}, f32[1,64,64]{2,1,0:T(8,128)}, u32[]{:S(2)}) copy-start(f32[1,64,64]{2,1,0:T(8,128)} %param.9) | copy-start | bytes 49156
  11.3 2.9 %copy-start.1 = (s32[1024]{0:T(1024)S(1)}, s32[1024]{0:T(1024)}, u32[]{:S(2)}) copy-start(s32[1024]{0:T(1024)} %order_ref.1) | copy-start | bytes 12292
